TPU v7x, 32 devices: a whole 2x2x4 slice. The times are simulated.
32 devices in a mesh: aa: 4 (over z), ba: 8 (over y, x, core).
Axes of the slice: x: 2, y: 2, z: 4, core: 2. Of those that a mesh axis runs over, the one named last changes fastest.
Arguments:
- corr_old: bfloat16 [14336, 28672], P('aa', 'ba'), may hold values from -0.19921875 to 0.19921875
- store_a: bfloat16 [2048, 14336], P('ba', 'aa'), may hold values from -6 to 6
- store_b: bfloat16 [2048, 28672], P('aa', 'ba'), may hold values from -6 to 6
- shuffle_order: int32 [2048], replicated, may hold values from 0 to 2047, each once
Outputs:
- current_comovement: bfloat16 [14336, 28672], P('aa', 'ba')
- source_multiplier: float32 [14336], P('aa')
- column_multiplier: float32 [28672], P('ba')
Inputs may be any that keep to these rules, and one draw needn't show every extreme that they name: `shuffle_order`: a permutation of the store's rows.
All inputs are finite; a program needn't handle non-finite values.
Results may differ from a plain program's by a relative error of at most 0.0068.
Values may be sent and summed in bfloat16 or wider, within the bound.
A program may use at most 192 MiB of HBM per device.

v0:
```python
import jax
import jax.numpy as jnp
from jax import lax
from jax.sharding import PartitionSpec as P

LEFT_NEURONS = 14336
RIGHT_NEURONS = 28672
GROUP = 1024
ITERS = 3


decay_factor = 0.5
regularizer_strength = 0.01


def contract(left, right):
    return lax.dot_general(
        left, right, (((0,), (0,)), ((), ())), preferred_element_type=jnp.float32
    )


def gibbs_tile(comovement):
    return jnp.exp(comovement.astype(jnp.float32) / regularizer_strength).astype(jnp.bfloat16)


def shards(corr_old, store_a, store_b, shuffle_order):
    rows_local = store_a.shape[0]
    chosen = jnp.zeros((shuffle_order.shape[0],), jnp.float32).at[shuffle_order[:GROUP]].set(1.0)
    first_row = lax.axis_index("ba") * rows_local
    kept_rows = lax.dynamic_slice_in_dim(chosen, first_row, rows_local, 0)
    masked_a = store_a * kept_rows[:, None].astype(jnp.bfloat16)
    source_patch = store_a.shape[1]
    tile_b = store_b.shape[1]
    whole_a = lax.all_gather(masked_a, "ba", axis=0, tiled=True)
    summed = contract(whole_a, lax.all_gather(store_b, "aa", axis=0, tiled=True))
    current_comovement = (
        decay_factor * corr_old.astype(jnp.float32) + (1.0 - decay_factor) / GROUP * summed
    ).astype(jnp.bfloat16)
    boltzmann_affinity = gibbs_tile(current_comovement)
    column_multiplier = jnp.ones((tile_b,), jnp.float32)
    source_multiplier = jnp.ones((source_patch,), jnp.float32)
    for step in range(ITERS):
        source_marginal = lax.psum(
            jnp.dot(
                boltzmann_affinity,
                column_multiplier.astype(jnp.bfloat16),
                preferred_element_type=jnp.float32,
            ),
            "ba",
        )
        source_multiplier = RIGHT_NEURONS / source_marginal
        column_marginal = lax.psum(
            jnp.dot(
                source_multiplier.astype(jnp.bfloat16),
                boltzmann_affinity,
                preferred_element_type=jnp.float32,
            ),
            "aa",
        )
        column_multiplier = LEFT_NEURONS / column_marginal
    return (current_comovement, source_multiplier, column_multiplier)


def solution(mesh):
    in_specs = (P("aa", "ba"), P("ba", "aa"), P("aa", "ba"), P())
    out_specs = (P("aa", "ba"), P("aa"), P("ba"))
    return jax.shard_map(shards, mesh=mesh, in_specs=in_specs, out_specs=out_specs, check_vma=False)
```

profile of v0, /device:TPU:0, one launch (start us, length us, event | category | flops | bytes accessed | tf_op | source)
XLA Modules:
  0.0 614.9 jit_solution(9755124289916794193)
XLA Ops:
  7.2 0.0 all-gather.5.cloned.1.call-start
  7.2 0.7 all-gather.5.cloned.1.call-update
  7.9 0.0 all-gather.3.cloned.1.call-start
  8.0 0.7 compare_select_fusion
  8.6 4.3 scatter_custom_fusion
  13.0 0.1 dynamic_slice.5
  13.0 2.9 broadcast_multiply_fusion
  16.0 0.0 all-gather.3.cloned.1.call-update
  16.0 248.8 %all-gather.5.cloned.1.call-done = bf16[2048,3584]{1,0:T(8,128)(2,1)} async-done(((bf16[512,3584]{1,0:T(8,128)(2,1)}), bf16[2048,3584]{1,0:T(8,128)(2,1)}) %all-gather.5.cloned.1.call-update) | async-done | bytes 14680080 | tf_op jit(solution)/shard_map/all_gather | solution.py:35
  264.8 81.7 %all-gather.3.cloned.1.call-done = bf16[2048,3584]{1,0:T(8,128)(2,1)} async-done(((bf16[256,3584]{1,0:T(8,128)(2,1)}), bf16[2048,3584]{1,0:T(8,128)(2,1)}) %all-gather.3.cloned.1.call-update) | async-done | bytes 14680080 | tf_op jit(solution)/shard_map/all_gather | solution.py:34
  346.5 66.4 %add_convert_fusion = bf16[3584,3584]{1,0:T(8,128)(2,1)} fusion(bf16[3584,3584]{1,0:T(8,128)(2,1)} %param.4, bf16[2048,3584]{1,0:T(8,128)(2,1)} %all-gather.3.cloned.1.call-done, bf16[2048,3584]{1,0:T(8,128)(2,1)} %all-gather.5.cloned.1.call-done), kind=kOutput, calls=%fused_computation.2 | convolution fusion | flops 52677574656 | bytes 80740352 | tf_op jit(solution)/shard_map/dot_general | solution.py:17
  412.9 12.5 %convolution_reduce_fusion.5 = f32[3584]{0:T(1024)S(1)} fusion(bf16[3584,3584]{1,0:T(8,128)(2,1)} %add_convert_fusion), kind=kOutput, calls=%fused_computation.8 | convolution fusion | flops 64225280 | bytes 25704448 | tf_op jit(solution)/shard_map/dot_general | solution.py:44
  425.4 23.5 %psum.42 = f32[3584]{0:T(1024)S(1)} all-reduce(f32[3584]{0:T(1024)S(1)} %convolution_reduce_fusion.5), channel_id=1, replica_groups=mesh['aa'=4,'ba'=8] {'ba'}, use_global_device_ids=true, to_apply=%region_1.0 | all-reduce | flops 3584 | bytes 28672 | tf_op jit(solution)/shard_map/psum | solution.py:43
  448.9 12.4 %convolution_reduce_fusion.4 = f32[3584]{0:T(1024)S(1)} fusion(bf16[3584,1]{0,1:T(2,128)(2,1)S(1)} %reshape.19, bf16[3584,3584]{1,0:T(8,128)(2,1)} %add_convert_fusion), kind=kOutput, calls=%fused_computation.7 | convolution fusion | flops 64225280 | bytes 25711616 | tf_op jit(solution)/shard_map/dot_general | solution.py:53
  461.3 18.7 %psum.43 = f32[3584]{0:T(1024)S(1)} all-reduce(f32[3584]{0:T(1024)S(1)} %convolution_reduce_fusion.4), channel_id=1, replica_groups=mesh['aa'=4,'ba'=8] {'aa'}, use_global_device_ids=true, to_apply=%region_2.0 | all-reduce | flops 3584 | bytes 28672 | tf_op jit(solution)/shard_map/psum | solution.py:52
  480.0 12.5 %convolution_reduce_fusion.3 = f32[3584]{0:T(1024)S(1)} fusion(bf16[3584,1]{0,1:T(2,128)(2,1)S(1)} %reshape.21, bf16[3584,3584]{1,0:T(8,128)(2,1)} %add_convert_fusion), kind=kOutput, calls=%fused_computation.6 | convolution fusion | flops 64225280 | bytes 25711616 | tf_op jit(solution)/shard_map/dot_general | solution.py:44
  492.5 22.5 %psum.44 = f32[3584]{0:T(1024)S(1)} all-reduce(f32[3584]{0:T(1024)S(1)} %convolution_reduce_fusion.3), channel_id=1, replica_groups=mesh['aa'=4,'ba'=8] {'ba'}, use_global_device_ids=true, to_apply=%region_3.0 | all-reduce | flops 3584 | bytes 28672 | tf_op jit(solution)/shard_map/psum | solution.py:43
  515.1 12.4 %convolution_reduce_fusion.2 = f32[3584]{0:T(1024)S(1)} fusion(bf16[3584,1]{0,1:T(2,128)(2,1)S(1)} %reshape.23, bf16[3584,3584]{1,0:T(8,128)(2,1)} %add_convert_fusion), kind=kOutput, calls=%fused_computation.5 | convolution fusion | flops 64225280 | bytes 25711616 | tf_op jit(solution)/shard_map/dot_general | solution.py:53
  527.5 15.5 %psum.45 = f32[3584]{0:T(1024)S(1)} all-reduce(f32[3584]{0:T(1024)S(1)} %convolution_reduce_fusion.2), channel_id=1, replica_groups=mesh['aa'=4,'ba'=8] {'aa'}, use_global_device_ids=true, to_apply=%region_4.0 | all-reduce | flops 3584 | bytes 28672 | tf_op jit(solution)/shard_map/psum | solution.py:52
  543.0 12.5 %convolution_reduce_fusion.1 = f32[3584]{0:T(1024)S(1)} fusion(bf16[3584,1]{0,1:T(2,128)(2,1)S(1)} %reshape.25, bf16[3584,3584]{1,0:T(8,128)(2,1)} %add_convert_fusion), kind=kOutput, calls=%fused_computation.4 | convolution fusion | flops 64225280 | bytes 25711616 | tf_op jit(solution)/shard_map/dot_general | solution.py:44
  555.5 22.6 %psum.46 = f32[3584]{0:T(1024)S(1)} all-reduce(f32[3584]{0:T(1024)S(1)} %convolution_reduce_fusion.1), channel_id=1, replica_groups=mesh['aa'=4,'ba'=8] {'ba'}, use_global_device_ids=true, to_apply=%region_5.0 | all-reduce | flops 3584 | bytes 28672 | tf_op jit(solution)/shard_map/psum | solution.py:43
  578.1 0.6 fusion.4
  578.7 12.4 %convolution_reduce_fusion = f32[3584]{0:T(1024)S(1)} fusion(bf16[3584,1]{0,1:T(2,128)(2,1)S(1)} %reshape.27, bf16[3584,3584]{1,0:T(8,128)(2,1)} %add_convert_fusion), kind=kOutput, calls=%fused_computation.3 | convolution fusion | flops 64225280 | bytes 25711616 | tf_op jit(solution)/shard_map/dot_general | solution.py:53
  591.1 16.3 %psum.47 = f32[3584]{0:T(1024)S(1)} all-reduce(f32[3584]{0:T(1024)S(1)} %convolution_reduce_fusion), channel_id=1, replica_groups=mesh['aa'=4,'ba'=8] {'aa'}, use_global_device_ids=true, to_apply=%region_6.0 | all-reduce | flops 3584 | bytes 28672 | tf_op jit(solution)/shard_map/psum | solution.py:52
  607.4 0.6 broadcast_divide_fusion
  (10 shorter events, 0.1 us)
Async XLA Ops:
  7.2 257.6 %all-gather.5.cloned.1.call-start = ((), (), s32[]{:S(2)}) async-start(), calls=%async_computation.1 | async-start | bytes 18350080 | tf_op jit(solution)/shard_map/all_gather | solution.py:35
  7.9 338.6 %all-gather.3.cloned.1.call-start = ((), (), s32[]{:S(2)}) async-start(), calls=%async_computation | async-start | bytes 16515072 | tf_op jit(solution)/shard_map/all_gather | solution.py:34
Sparse Core Ops, SparseCore 0:
  9.6 255.1 all-gather.4
  267.3 79.1 all-gather.2
where the time goes:
time: 615 us
  waiting for transfers between devices  331 us (54%)
  matrix products  141 us (23%)
  blocking collectives  119 us (19%)
  between operations  14.1 us (2%)
    all_gather x1, waiting for transfers between devices, shards(): lax.all_gather(store_b, 'aa', axis=0, tiled=True)  249 us
    all_gather x1, waiting for transfers between devices, shards(): whole_a = lax.all_gather(masked_a, 'ba', axis=0, tiled=True)  81.7 us
    psum x3, blocking collectives, shards(): lax.psum(jnp.dot(boltzmann_affinity, column_multiplier.astype(jnp.bfloat1...  68.6 us
    dot_general x1, matrix products, contract(): lax.dot_general(left, right, (((0,), (0,)), ((), ())), preferred_element_...  66.4 us
    psum x3, blocking collectives, shards(): lax.psum(jnp.dot(source_multiplier.astype(jnp.bfloat16), boltzmann_affini...  50.6 us
    dot_general x3, matrix products, shards(): jnp.dot(boltzmann_affinity, column_multiplier.astype(jnp.bfloat16), prefe...  37.5 us
    dot_general x3, matrix products, shards(): jnp.dot(source_multiplier.astype(jnp.bfloat16), boltzmann_affinity, prefe...  37.1 us
  transfers between devices with their start and end apart: 2, of which 2 were waited for; matrix products, arithmetic and copies ran while one was open for 1% of the time, Pallas kernels for 0%

commit v1 on v0

v1 whole, which is shorter than its diff:
```python
import functools

import jax
import jax.numpy as jnp
from jax import lax
from jax.experimental import pallas as pl
from jax.experimental.pallas import tpu as pltpu
from jax.sharding import PartitionSpec as P

GROUP = 1024
ITERS = 3
MESH = pl.DeviceIdType.MESH

decay_factor = 0.5
regularizer_strength = 0.01

CHUNK = 256
AHEAD = 3
FIRST = 4


def contract(left, right):
    return lax.dot_general(
        left, right, (((0,), (0,)), ((), ())), preferred_element_type=jnp.float32
    )


def kernel(na, nb, S, W, bp, ap, corr, com, src_out, col_out,
           K, AT, B, cbuf, obuf, apart, aown, rs, rowx, colx,
           b_send, b_recv, b_loc, a_send, a_recv, f_send, p_sem, a_loc,
           c_sem, o_sem, r_send, r_recv, k_send, k_recv):
    ia, ib = lax.axis_index("aa"), lax.axis_index("ba")
    Q = W // CHUNK
    H = W // 2
    R = 512 if W % 512 == 0 else 256
    c = lax.rem(ib, 2)
    sa = ib // 2
    sib = ib + 1 - 2 * c

    barrier = pltpu.get_barrier_semaphore()
    for d in range(1, na):
        pl.semaphore_signal(barrier, inc=1, device_id=(lax.rem(ia + d, na), ib), device_id_type=MESH)
    for d in range(1, nb):
        pl.semaphore_signal(barrier, inc=1, device_id=(ia, lax.rem(ib + d, nb)), device_id_type=MESH)

    def corr_copy(q):
        slot = lax.rem(q, 2)
        return pltpu.make_async_copy(
            corr.at[:, pl.ds(pl.multiple_of(q * CHUNK, CHUNK), CHUNK)], cbuf.at[slot], c_sem.at[slot])

    def out_copy(q):
        slot = lax.rem(q, 2)
        return pltpu.make_async_copy(
            obuf.at[slot], com.at[:, pl.ds(pl.multiple_of(q * CHUNK, CHUNK), CHUNK)], o_sem.at[slot])

    def half(ref, h):
        return ref.at[:, pl.ds(pl.multiple_of(h * H, 128), H)]

    own_a = pltpu.make_async_copy(half(ap, c), aown, a_loc)
    own_a.start()
    corr_copy(0).start()
    rs[...] = jnp.zeros_like(rs)
    pl.semaphore_wait(barrier, na + nb - 2)

    part = pltpu.make_async_remote_copy(
        src_ref=half(ap, 1 - c), dst_ref=apart, send_sem=p_sem.at[0], recv_sem=p_sem.at[1],
        device_id=(ia, sib), device_id_type=MESH)
    part.start()

    def b_slot(s, t):
        return B.at[t, pl.ds(pl.multiple_of(s * S, 16), S)]

    def b_src(t):
        return bp.at[:, pl.ds(pl.multiple_of(t * CHUNK, CHUNK), CHUNK)]

    def b_copy(up, s, t, source):
        return pltpu.make_async_remote_copy(
            src_ref=source, dst_ref=b_slot(s, t), send_sem=b_send.at[up, s, t], recv_sem=b_recv.at[s, t],
            device_id=(ia + 1 if up == 0 else ia - 1, ib), device_id_type=MESH)

    def b_own(t):
        @pl.when(ia < na - 1)
        def _():
            b_copy(0, ia, t, b_src(t)).start()

        @pl.when(ia > 0)
        def _():
            b_copy(1, ia, t, b_src(t)).start()

        pltpu.make_async_copy(b_src(t), b_slot(ia, t), b_loc.at[t]).start()

    def comm(t):
        @pl.when(t + AHEAD < Q)
        def _():
            b_own(t + AHEAD)

        for d in range(1, na):
            @pl.when(ia - d >= 0)
            def _():
                s = ia - d
                b_copy(0, s, t, b_slot(s, t)).wait_recv()

                @pl.when(ia < na - 1)
                def _():
                    b_copy(0, s, t, b_slot(s, t)).start()

            @pl.when(ia + d < na)
            def _():
                s = ia + d
                b_copy(1, s, t, b_slot(s, t)).wait_recv()

                @pl.when(ia > 0)
                def _():
                    b_copy(1, s, t, b_slot(s, t)).start()

        pltpu.make_async_copy(b_src(t), b_slot(ia, t), b_loc.at[t]).wait()

    def a_slot(p, h):
        return K.at[pl.ds(pl.multiple_of(p * S, 16), S), pl.ds(pl.multiple_of(h * H, 128), H)]

    def a_copy(p, d):
        return pltpu.make_async_remote_copy(
            src_ref=a_slot(p, c), dst_ref=a_slot(p, c), send_sem=a_send.at[d], recv_sem=a_recv.at[p, c],
            device_id=(ia, lax.rem(ib + 2 * d, nb)), device_id_type=MESH)

    def a_forward(p, h):
        return pltpu.make_async_remote_copy(
            src_ref=a_slot(p, h), dst_ref=a_slot(p, h), send_sem=f_send.at[p], recv_sem=a_recv.at[p, h],
            device_id=(ia, sib), device_id_type=MESH)

    for t in range(min(AHEAD, Q)):
        b_own(t)
    own_a.wait()
    part.wait()
    a_slot(sa, c)[...] = aown[...] + apart[...]
    for d in range(1, na):
        a_copy(sa, d).start()
    a_forward(sa, c).start()

    def early(t, carry):
        comm(t)
        return carry

    lax.fori_loop(0, FIRST, early, 0)
    for d in range(1, na):
        p = lax.rem(sa + na - d, na)
        a_copy(p, d).wait_recv()
        a_forward(p, c).start()
    for p in range(na):
        a_forward(p, 1 - c).wait_recv()

    def turn(i, carry):
        cols = pl.ds(pl.multiple_of(i * 256, 256), 256)
        AT[cols, :] = K[0:na * S, cols].T
        return carry

    lax.fori_loop(0, W // 256, turn, 0)
    for d in range(1, na):
        a_copy(sa, d).wait_send()
    for p in range(na):
        a_forward(p, c).wait_send()

    ones = jnp.ones((16, CHUNK), jnp.bfloat16)

    def compute(q, carry):
        slot = lax.rem(q, 2)
        corr_copy(q).wait()

        @pl.when(q + 1 < Q)
        def _():
            corr_copy(q + 1).start()

        @pl.when(q >= 2)
        def _():
            out_copy(q - 2).wait()

        cols = pl.ds(pl.multiple_of(q * CHUNK, CHUNK), CHUNK)

        def block(r, carry):
            rows = pl.ds(pl.multiple_of(r * R, R), R)
            acc = jnp.dot(AT[rows, :], B[q], preferred_element_type=jnp.float32)
            cm = (decay_factor * cbuf[slot, rows, :].astype(jnp.float32)
                  + (1.0 - decay_factor) / GROUP * acc).astype(jnp.bfloat16)
            obuf[slot, rows, :] = cm
            e = jnp.exp(cm.astype(jnp.float32) * (1.0 / regularizer_strength)).astype(jnp.bfloat16)
            K[rows, cols] = e
            rs[:, rows] += lax.dot_general(
                ones, e, (((1,), (1,)), ((), ())), preferred_element_type=jnp.float32)
            return carry

        lax.fori_loop(0, W // R, block, 0)
        out_copy(q).start()
        return carry

    def done(t):
        return jnp.maximum(jnp.minimum(2 * (t - FIRST + 1), t), 0)

    def main(t, carry):
        comm(t)
        lax.fori_loop(done(t - 1), done(t), compute, 0)
        return carry

    lax.fori_loop(FIRST, Q, main, 0)
    lax.fori_loop(min(2 * (Q - FIRST), Q - 1), Q, compute, 0)

    def exchange(it, n, me, peer, buf, send, recv, partial):
        buf[it * n + me] = partial

        def copy(owner, d):
            return pltpu.make_async_remote_copy(
                src_ref=buf.at[it * n + owner], dst_ref=buf.at[it * n + owner],
                send_sem=send.at[it, d], recv_sem=recv.at[it, owner],
                device_id=peer(lax.rem(me + d, n)), device_id_type=MESH)

        for d in range(1, n):
            copy(me, d).start()
        for d in range(1, n):
            copy(lax.rem(me + n - d, n), d).wait_recv()
        total = buf[it * n]
        for j in range(1, n):
            total = total + buf[it * n + j]
        for d in range(1, n):
            copy(me, d).wait_send()
        return total

    def row_pass(colm):
        lhs = jnp.broadcast_to(colm, (16, W)).astype(jnp.bfloat16)

        def body(r, carry):
            rows = pl.ds(pl.multiple_of(r * R, R), R)
            rs[:, rows] = lax.dot_general(
                lhs, K[rows, :], (((1,), (1,)), ((), ())), preferred_element_type=jnp.float32)
            return carry

        lax.fori_loop(0, W // R, body, 0)
        return rs[0:1, :]

    def col_pass(srcm):
        lhs = jnp.broadcast_to(srcm, (16, W)).astype(jnp.bfloat16)

        def body(r, carry):
            cols = pl.ds(pl.multiple_of(r * R, R), R)
            rs[:, cols] = jnp.dot(lhs, K[:, cols], preferred_element_type=jnp.float32)
            return carry

        lax.fori_loop(0, W // R, body, 0)
        return rs[0:1, :]

    partial = rs[0:1, :]
    for it in range(ITERS):
        if it > 0:
            partial = row_pass(col_out[...])
        row = exchange(it, nb, ib, lambda j: (ia, j), rowx, r_send, r_recv, partial)
        src_out[...] = (nb * W) / row
        partial = col_pass(src_out[...])
        col = exchange(it, na, ia, lambda j: (j, ib), colx, k_send, k_recv, partial)
        col_out[...] = (na * W) / col

    for q in range(max(Q - 2, 0), Q):
        out_copy(q).wait()

    def drain(t, carry):
        for s in range(na):
            @pl.when((ia < na - 1) & (s <= ia))
            def _():
                b_copy(0, s, t, b_slot(s, t)).wait_send()

            @pl.when((ia > 0) & (s >= ia))
            def _():
                b_copy(1, s, t, b_slot(s, t)).wait_send()
        return carry

    lax.fori_loop(0, Q, drain, 0)


def fused(na, nb, S, W, bp, ap, corr):
    Q = W // CHUNK
    dma = pltpu.SemaphoreType.DMA
    any_space = pl.BlockSpec(memory_space=pl.ANY)
    vmem = pl.BlockSpec(memory_space=pltpu.VMEM)
    return pl.pallas_call(
        functools.partial(kernel, na, nb, S, W),
        out_shape=(
            jax.ShapeDtypeStruct((W, W), jnp.bfloat16),
            jax.ShapeDtypeStruct((1, W), jnp.float32),
            jax.ShapeDtypeStruct((1, W), jnp.float32),
        ),
        in_specs=[any_space] * 3,
        out_specs=(any_space, vmem, vmem),
        scratch_shapes=[
            pltpu.VMEM((W, W), jnp.bfloat16),
            pltpu.VMEM((W, na * S), jnp.bfloat16),
            pltpu.VMEM((Q, na * S, CHUNK), jnp.bfloat16),
            pltpu.VMEM((2, W, CHUNK), jnp.bfloat16),
            pltpu.VMEM((2, W, CHUNK), jnp.bfloat16),
            pltpu.VMEM((S, W // 2), jnp.bfloat16),
            pltpu.VMEM((S, W // 2), jnp.bfloat16),
            pltpu.VMEM((16, W), jnp.float32),
            pltpu.VMEM((ITERS * nb, 1, W), jnp.float32),
            pltpu.VMEM((ITERS * na, 1, W), jnp.float32),
            dma((2, na, Q)), dma((na, Q)), dma((Q,)),
            dma((na,)), dma((na, 2)), dma((na,)), dma((2,)), dma,
            dma((2,)), dma((2,)),
            dma((ITERS, nb)), dma((ITERS, nb)), dma((ITERS, na)), dma((ITERS, na)),
        ],
        compiler_params=pltpu.CompilerParams(
            collective_id=0, has_side_effects=True, vmem_limit_bytes=60 * 2**20),
        cost_estimate=pl.CostEstimate(
            flops=2 * GROUP * W * W, bytes_accessed=4 * W * W, transcendentals=W * W),
    )(bp, ap, corr)


def general(na, nb, corr_old, store_a, store_b, shuffle_order):
    rows_local = store_a.shape[0]
    chosen = jnp.zeros((shuffle_order.shape[0],), jnp.float32).at[shuffle_order[:GROUP]].set(1.0)
    kept_rows = lax.dynamic_slice_in_dim(chosen, lax.axis_index("ba") * rows_local, rows_local, 0)
    masked_a = store_a * kept_rows[:, None].astype(jnp.bfloat16)
    whole_a = lax.all_gather(masked_a, "ba", axis=0, tiled=True)
    summed = contract(whole_a, lax.all_gather(store_b, "aa", axis=0, tiled=True))
    com = (
        decay_factor * corr_old.astype(jnp.float32) + (1.0 - decay_factor) / GROUP * summed
    ).astype(jnp.bfloat16)
    K = jnp.exp(com.astype(jnp.float32) / regularizer_strength).astype(jnp.bfloat16)
    W = store_b.shape[1]
    col = jnp.ones((W,), jnp.float32)
    src = jnp.ones((store_a.shape[1],), jnp.float32)
    for _ in range(ITERS):
        src = nb * W / lax.psum(
            jnp.dot(K, col.astype(jnp.bfloat16), preferred_element_type=jnp.float32), "ba")
        col = na * store_a.shape[1] / lax.psum(
            jnp.dot(src.astype(jnp.bfloat16), K, preferred_element_type=jnp.float32), "aa")
    return com, src[None], col[None]


def shards(na, nb, corr_old, store_a, store_b, shuffle_order):
    ia, ib = lax.axis_index("aa"), lax.axis_index("ba")
    L, La = store_b.shape[0], store_a.shape[0]
    W = store_b.shape[1]
    step = max(16, 128 // na)
    S = -(-(GROUP // na + 32) // step) * step
    group = shuffle_order[:GROUP]
    owner = group // L
    order = jnp.arange(GROUP)

    def slots(seg):
        mine = owner == seg
        rank = jnp.sum((mine[None, :] & (order[None, :] < order[:, None])).astype(jnp.int32), axis=1)
        hit = mine[None, :] & (rank[None, :] == jnp.arange(S)[:, None])
        return jnp.sum(jnp.where(hit, group[None, :] + 1, 0), axis=1) - 1

    def pick(rows, first, store):
        hot = (rows[:, None] == first + jnp.arange(store.shape[0])[None, :]).astype(jnp.bfloat16)
        return jnp.dot(hot, store, preferred_element_type=jnp.float32).astype(jnp.bfloat16)

    fits = jnp.max(jnp.sum((owner[:, None] == jnp.arange(na)[None, :]).astype(jnp.int32), axis=0)) <= S

    def fast(corr_old, store_a, store_b, shuffle_order):
        bp = pick(slots(ia), ia * L, store_b)
        ap = pick(slots(ib // 2), ib * La, store_a)
        return fused(na, nb, S, W, bp, ap, corr_old)

    com, src, col = lax.cond(
        fits, fast, functools.partial(general, na, nb), corr_old, store_a, store_b, shuffle_order)
    return com, src[0], col[0]


def solution(mesh):
    na, nb = mesh.shape["aa"], mesh.shape["ba"]
    in_specs = (P("aa", "ba"), P("ba", "aa"), P("aa", "ba"), P())
    out_specs = (P("aa", "ba"), P("aa"), P("ba"))
    return jax.shard_map(
        functools.partial(shards, na, nb), mesh=mesh, in_specs=in_specs, out_specs=out_specs, check_vma=False)
```

time: 615 us -> 304 us (0.49)
  waiting for transfers between devices: 331 us -> 0 us
  Pallas kernels: 0 us -> 254 us
  matrix products: 141 us -> 8.23 us
  blocking collectives: 119 us -> 0 us
  local copies, waits for them, and re-layouts: 4.45 us -> 21.4 us
    all_gather x2 -> x0, waiting for transfers between devices: 330 us -> none  [the longest x1 249 us: shards(): lax.all_gather(store_b, 'aa', axis=0, tiled=True)]
    pallas_call x0 -> x1, Pallas kernels: none -> 254 us  [fused(): pl.pallas_call(functools.partial(kernel, na, nb, S, W), out_shape=(jax.Sh...]
    dot_general x7 -> x2, matrix products: 141 us -> 8.23 us  [pick(): jnp.dot(hot, store, preferred_element_type=jnp.float32).astype(jnp.bfloat16)]
    psum x6 -> x0, blocking collectives: 119 us -> none  [the longest x3 68.6 us: shards(): lax.psum(jnp.dot(boltzmann_affinity, column_multiplier.astype(jnp.bfloat1...]
    unnamed x0 -> x7, local copies, waits for them, and re-layouts: none -> 21.4 us
  transfers between devices with their start and end apart: 2 -> 0, of which waited for: 2 -> 0; matrix products, arithmetic and copies ran while one was open for 1% -> 0% of each run, Pallas kernels for 0% -> 0%
where the time goes in v1:
time: 304 us
  Pallas kernels  254 us (84%)
  local copies, waits for them, and re-layouts  21.4 us (7%)
  between operations  14.7 us (5%)
  matrix products  8.23 us (3%)
  other arithmetic  5.73 us (2%)
    pallas_call x1, Pallas kernels, fused(): pl.pallas_call(functools.partial(kernel, na, nb, S, W), out_shape=(jax.Sh...  254 us
    unnamed x7, local copies, waits for them, and re-layouts  21.4 us
    dot_general x2, matrix products, pick(): jnp.dot(hot, store, preferred_element_type=jnp.float32).astype(jnp.bfloat16)  8.23 us

profile of v1, /device:TPU:0, one launch (start us, length us, event | category | flops | bytes accessed | tf_op | source)
XLA Modules:
  0.0 303.9 jit_solution(2025624348359274180)
XLA Ops:
  7.2 0.7 fusion.15
  7.9 0.0 copy-start
  7.9 0.6 copy-done
  8.5 0.1 convert_reduce_fusion.2
  8.6 0.6 reduce_max.9
  9.9 266.3 %conditional.1 = (bf16[3584,3584]{1,0:T(8,128)(2,1)}, f32[3584]{0:T(1024)S(1)}, f32[3584]{0:T(1024)S(1)}) conditional(s32[]{:T(128)} %convert_element_type.52, (bf16[3584,3584]{1,0:T(8,128)(2,1)}, s32[2048]{0:T(1024)}, bf16[256,3584]{1,0:T(8,128)(2,1)}, bf16[512,3584]{1,0:T(8,128)(2,1)}) %tuple.19, (s32[]{:T(128)}, s32[1024]{0:T(1024)}, ...), branch_computations={%region_2.10_spmd, %region_10.15_spmd} | conditional | flops 53063917568 | bytes 343684800 | solution.py:362
  10.1 0.7 broadcast_compare_fusion.1
  10.9 1.5 convert_reduce_fusion
  12.3 0.6 select_reduce_fusion
  12.9 4.6 %convolution_convert_fusion.1.bp = bf16[288,3584]{1,0:T(8,128)(2,1)} fusion(bf16[512,3584]{1,0:T(8,128)(2,1)} %get-tuple-element.38, s32[512]{0:T(512)S(1)} %iota_add_fusion, s32[288]{0:T(512)S(1)} %broadcast_add_fusion.2), kind=kOutput, calls=%fused_computation.2 | convolution fusion | flops 1058144256 | bytes 5737600 | tf_op jit(solution)/shard_map/cond/branch_1_fun/dot_general | solution.py:353
  17.6 3.6 %convolution_convert_fusion.ap = bf16[288,3584]{1,0:T(8,128)(2,1)} fusion(bf16[256,3584]{1,0:T(8,128)(2,1)} %get-tuple-element.41, s32[256]{0:T(256)S(1)} %iota_add_fusion.1, s32[288]{0:T(512)S(1)} %broadcast_add_fusion.1), kind=kOutput, calls=%fused_computation.1 | convolution fusion | flops 529588224 | bytes 3901568 | tf_op jit(solution)/shard_map/cond/branch_1_fun/dot_general | solution.py:353
  21.2 253.5 %branch_1_fun.1 = (bf16[3584,3584]{1,0:T(8,128)(2,1)}, f32[1,3584]{1,0:T(1,128)}, f32[1,3584]{1,0:T(1,128)}) custom-call(bf16[288,3584]{1,0:T(8,128)(2,1)} %convolution_convert_fusion.1.bp, bf16[288,3584]{1,0:T(8,128)(2,1)} %convolution_convert_fusion.ap, bf16[3584,3584]{1,0:T(8,128)(2,1)} %get-tuple-element.42.corr), custom_call_target="tpu_custom_call" | custom-call | flops 26306674688 | bytes 51380224 | tf_op jit(solution)/shard_map/cond/branch_1_fun/pallas_call | solution.py:281
  274.7 0.8 reduce
  275.4 0.8 reduce.1
  276.2 0.0 copy-start.1
  276.2 0.0 copy-start.2
  276.2 20.8 %copy.20 = bf16[3584,3584]{1,0:T(8,128)(2,1)} copy(bf16[3584,3584]{1,0:T(8,128)(2,1)} %get-tuple-element.71) | data formatting | bytes 51380224
  297.0 0.0 copy-done.1
  297.0 0.0 copy-done.2
  (6 shorter events, 0.0 us)
Async XLA Ops:
  7.9 0.6 copy-start
  276.2 20.9 %copy-start.1 = (f32[3584]{0:T(1024)}, f32[3584]{0:T(1024)S(1)}, u32[]{:S(2)}) copy-start(f32[3584]{0:T(1024)S(1)} %get-tuple-element.72) | copy-start | bytes 43012
  276.2 20.8 %copy-start.2 = (f32[3584]{0:T(1024)}, f32[3584]{0:T(1024)S(1)}, u32[]{:S(2)}) copy-start(f32[3584]{0:T(1024)S(1)} %get-tuple-element.73) | copy-start | bytes 43012

commit v2 on v1

--- a/solution.py
+++ b/solution.py
@@ -15,8 +15,7 @@
 regularizer_strength = 0.01
 
 CHUNK = 256
-AHEAD = 3
-FIRST = 4
+FIRST = 2
 
 
 def contract(left, right):
@@ -25,9 +24,9 @@
     )
 
 
-def kernel(na, nb, S, W, bp, ap, corr, com, src_out, col_out,
-           K, AT, B, cbuf, obuf, apart, aown, rs, rowx, colx,
-           b_send, b_recv, b_loc, a_send, a_recv, f_send, p_sem, a_loc,
+def kernel(na, nb, S, W, hot_b, hot_a, store_b, store_a, corr, com, src_out, col_out,
+           K, AT, B, cbuf, obuf, apart, asend, rs, rowx, colx,
+           b_send, b_recv, a_send, a_recv, f_send, p_sem, l_sem,
            c_sem, o_sem, r_send, r_recv, k_send, k_recv):
     ia, ib = lax.axis_index("aa"), lax.axis_index("ba")
     Q = W // CHUNK
@@ -53,25 +52,36 @@
         return pltpu.make_async_copy(
             obuf.at[slot], com.at[:, pl.ds(pl.multiple_of(q * CHUNK, CHUNK), CHUNK)], o_sem.at[slot])
 
-    def half(ref, h):
-        return ref.at[:, pl.ds(pl.multiple_of(h * H, 128), H)]
-
-    own_a = pltpu.make_async_copy(half(ap, c), aown, a_loc)
-    own_a.start()
+    L, La = store_b.shape[0], store_a.shape[0]
+    rows_b = pl.ds(na * S, L)
+    rows_a = pl.ds(na * S + L, La)
+    load_a = pltpu.make_async_copy(store_a, K.at[rows_a], l_sem.at[0])
+    load_b = pltpu.make_async_copy(store_b, K.at[rows_b], l_sem.at[1])
+    load_a.start()
+    load_b.start()
     corr_copy(0).start()
     rs[...] = jnp.zeros_like(rs)
+
+    def pick_a(h, dst):
+        def body(i, carry):
+            cols = pl.ds(pl.multiple_of(h * H + i * 128, 128), 128)
+            dst[:, pl.ds(pl.multiple_of(i * 128, 128), 128)] = jnp.dot(
+                hot_a[...], K[rows_a, cols], preferred_element_type=jnp.float32).astype(jnp.bfloat16)
+            return carry
+
+        lax.fori_loop(0, H // 128, body, 0)
+
+    load_a.wait()
+    pick_a(1 - c, asend)
     pl.semaphore_wait(barrier, na + nb - 2)
 
     part = pltpu.make_async_remote_copy(
-        src_ref=half(ap, 1 - c), dst_ref=apart, send_sem=p_sem.at[0], recv_sem=p_sem.at[1],
+        src_ref=asend, dst_ref=apart, send_sem=p_sem.at[0], recv_sem=p_sem.at[1],
         device_id=(ia, sib), device_id_type=MESH)
     part.start()
 
     def b_slot(s, t):
         return B.at[t, pl.ds(pl.multiple_of(s * S, 16), S)]
-
-    def b_src(t):
-        return bp.at[:, pl.ds(pl.multiple_of(t * CHUNK, CHUNK), CHUNK)]
 
     def b_copy(up, s, t, source):
         return pltpu.make_async_remote_copy(
@@ -79,41 +89,47 @@
             device_id=(ia + 1 if up == 0 else ia - 1, ib), device_id_type=MESH)
 
     def b_own(t):
+        cols = pl.ds(pl.multiple_of(t * CHUNK, CHUNK), CHUNK)
+        B[t, pl.ds(pl.multiple_of(ia * S, 16), S), :] = jnp.dot(
+            hot_b[...], K[rows_b, cols], preferred_element_type=jnp.float32).astype(jnp.bfloat16)
+
         @pl.when(ia < na - 1)
         def _():
-            b_copy(0, ia, t, b_src(t)).start()
+            b_copy(0, ia, t, b_slot(ia, t)).start()
 
         @pl.when(ia > 0)
         def _():
-            b_copy(1, ia, t, b_src(t)).start()
-
-        pltpu.make_async_copy(b_src(t), b_slot(ia, t), b_loc.at[t]).start()
-
-    def comm(t):
-        @pl.when(t + AHEAD < Q)
-        def _():
-            b_own(t + AHEAD)
+            b_copy(1, ia, t, b_slot(ia, t)).start()
+
+    last = 2 * (na - 1)
+
+    def inside(i, d):
+        return (i >= 2 * d) & (i < Q + 2 * d)
+
+    def comm(i):
+        @pl.when(inside(i, 0))
+        def _():
+            b_own(jnp.minimum(i, Q - 1))
 
         for d in range(1, na):
-            @pl.when(ia - d >= 0)
-            def _():
-                s = ia - d
-                b_copy(0, s, t, b_slot(s, t)).wait_recv()
+            u = jnp.clip(i - 2 * d, 0, Q - 1)
+
+            def below(u=u, s=ia - d):
+                b_copy(0, s, u, b_slot(s, u)).wait_recv()
 
                 @pl.when(ia < na - 1)
                 def _():
-                    b_copy(0, s, t, b_slot(s, t)).start()
-
-            @pl.when(ia + d < na)
-            def _():
-                s = ia + d
-                b_copy(1, s, t, b_slot(s, t)).wait_recv()
+                    b_copy(0, s, u, b_slot(s, u)).start()
+
+            def above(u=u, s=ia + d):
+                b_copy(1, s, u, b_slot(s, u)).wait_recv()
 
                 @pl.when(ia > 0)
                 def _():
-                    b_copy(1, s, t, b_slot(s, t)).start()
-
-        pltpu.make_async_copy(b_src(t), b_slot(ia, t), b_loc.at[t]).wait()
+                    b_copy(1, s, u, b_slot(s, u)).start()
+
+            pl.when(inside(i, d) & (ia - d >= 0))(below)
+            pl.when(inside(i, d) & (ia + d < na))(above)
 
     def a_slot(p, h):
         return K.at[pl.ds(pl.multiple_of(p * S, 16), S), pl.ds(pl.multiple_of(h * H, 128), H)]
@@ -128,20 +144,28 @@
             src_ref=a_slot(p, h), dst_ref=a_slot(p, h), send_sem=f_send.at[p], recv_sem=a_recv.at[p, h],
             device_id=(ia, sib), device_id_type=MESH)
 
-    for t in range(min(AHEAD, Q)):
-        b_own(t)
-    own_a.wait()
+    load_b.wait()
+
+    def early(t, carry):
+        comm(t)
+        return carry
+
+    lax.fori_loop(0, 2, early, 0)
     part.wait()
-    a_slot(sa, c)[...] = aown[...] + apart[...]
+
+    def merge(i, carry):
+        here = pl.ds(pl.multiple_of(i * 128, 128), 128)
+        cols = pl.ds(pl.multiple_of(c * H + i * 128, 128), 128)
+        own = jnp.dot(hot_a[...], K[rows_a, cols], preferred_element_type=jnp.float32)
+        K[pl.ds(pl.multiple_of(sa * S, 16), S), cols] = own.astype(jnp.bfloat16) + apart[:, here]
+        return carry
+
+    lax.fori_loop(0, H // 128, merge, 0)
     for d in range(1, na):
         a_copy(sa, d).start()
     a_forward(sa, c).start()
 
-    def early(t, carry):
-        comm(t)
-        return carry
-
-    lax.fori_loop(0, FIRST, early, 0)
+    lax.fori_loop(2, last + FIRST, early, 0)
     for d in range(1, na):
         p = lax.rem(sa + na - d, na)
         a_copy(p, d).wait_recv()
@@ -193,15 +217,14 @@
         return carry
 
     def done(t):
-        return jnp.maximum(jnp.minimum(2 * (t - FIRST + 1), t), 0)
+        return jnp.minimum(2 * (t - FIRST + 1), t + 1)
 
     def main(t, carry):
-        comm(t)
+        comm(t + last)
         lax.fori_loop(done(t - 1), done(t), compute, 0)
         return carry
 
     lax.fori_loop(FIRST, Q, main, 0)
-    lax.fori_loop(min(2 * (Q - FIRST), Q - 1), Q, compute, 0)
 
     def exchange(it, n, me, peer, buf, send, recv, partial):
         buf[it * n + me] = partial
@@ -273,7 +296,7 @@
     lax.fori_loop(0, Q, drain, 0)
 
 
-def fused(na, nb, S, W, bp, ap, corr):
+def fused(na, nb, S, W, hot_b, hot_a, store_b, store_a, corr):
     Q = W // CHUNK
     dma = pltpu.SemaphoreType.DMA
     any_space = pl.BlockSpec(memory_space=pl.ANY)
@@ -285,7 +308,7 @@
             jax.ShapeDtypeStruct((1, W), jnp.float32),
             jax.ShapeDtypeStruct((1, W), jnp.float32),
         ),
-        in_specs=[any_space] * 3,
+        in_specs=[vmem] * 2 + [any_space] * 3,
         out_specs=(any_space, vmem, vmem),
         scratch_shapes=[
             pltpu.VMEM((W, W), jnp.bfloat16),
@@ -298,8 +321,8 @@
             pltpu.VMEM((16, W), jnp.float32),
             pltpu.VMEM((ITERS * nb, 1, W), jnp.float32),
             pltpu.VMEM((ITERS * na, 1, W), jnp.float32),
-            dma((2, na, Q)), dma((na, Q)), dma((Q,)),
-            dma((na,)), dma((na, 2)), dma((na,)), dma((2,)), dma,
+            dma((2, na, Q)), dma((na, Q)),
+            dma((na,)), dma((na, 2)), dma((na,)), dma((2,)), dma((2,)),
             dma((2,)), dma((2,)),
             dma((ITERS, nb)), dma((ITERS, nb)), dma((ITERS, na)), dma((ITERS, na)),
         ],
@@ -307,7 +330,7 @@
             collective_id=0, has_side_effects=True, vmem_limit_bytes=60 * 2**20),
         cost_estimate=pl.CostEstimate(
             flops=2 * GROUP * W * W, bytes_accessed=4 * W * W, transcendentals=W * W),
-    )(bp, ap, corr)
+    )(hot_b, hot_a, store_b, store_a, corr)
 
 
 def general(na, nb, corr_old, store_a, store_b, shuffle_order):
@@ -348,17 +371,15 @@
         hit = mine[None, :] & (rank[None, :] == jnp.arange(S)[:, None])
         return jnp.sum(jnp.where(hit, group[None, :] + 1, 0), axis=1) - 1
 
-    def pick(rows, first, store):
-        hot = (rows[:, None] == first + jnp.arange(store.shape[0])[None, :]).astype(jnp.bfloat16)
-        return jnp.dot(hot, store, preferred_element_type=jnp.float32).astype(jnp.bfloat16)
+    def hot(rows, first, n):
+        return (rows[:, None] == first + jnp.arange(n)[None, :]).astype(jnp.bfloat16)
 
     fits = jnp.max(jnp.sum((owner[:, None] == jnp.arange(na)[None, :]).astype(jnp.int32), axis=0)) <= S
 
     def fast(corr_old, store_a, store_b, shuffle_order):
-        bp = pick(slots(ia), ia * L, store_b)
-        ap = pick(slots(ib // 2), ib * La, store_a)
-        return fused(na, nb, S, W, bp, ap, corr_old)
-
+        return fused(
+            na, nb, S, W, hot(slots(ia), ia * L, L), hot(slots(ib // 2), ib * La, La),
+            store_b, store_a, corr_old)
     com, src, col = lax.cond(
         fits, fast, functools.partial(general, na, nb), corr_old, store_a, store_b, shuffle_order)
     return com, src[0], col[0]

time: 304 us -> 252 us (0.83)
  Pallas kernels: 254 us -> 208 us
  matrix products: 8.23 us -> 0 us
    pallas_call x1, Pallas kernels: 254 us -> 208 us  [fused(): pl.pallas_call(functools.partial(kernel, na, nb, S, W), out_shape=(jax.Sh...]
    dot_general x2 -> x0, matrix products: 8.23 us -> none  [pick(): jnp.dot(hot, store, preferred_element_type=jnp.float32).astype(jnp.bfloat16)]
where the time goes in v2:
time: 252 us
  Pallas kernels  208 us (83%)
  local copies, waits for them, and re-layouts  21.4 us (8%)
  between operations  14.7 us (6%)
  other arithmetic  7.32 us (3%)
    pallas_call x1, Pallas kernels, fused(): pl.pallas_call(functools.partial(kernel, na, nb, S, W), out_shape=(jax.Sh...  208 us
    unnamed x7, local copies, waits for them, and re-layouts  21.4 us

profile of v2, /device:TPU:0, one launch (start us, length us, event | category | flops | bytes accessed | tf_op | source)
XLA Modules:
  0.0 252.0 jit_solution(6774501673484194685)
XLA Ops:
  7.2 0.7 fusion.9
  7.9 0.0 copy-start
  7.9 0.6 copy-done
  8.5 0.1 convert_reduce_fusion.2
  8.6 0.6 reduce_max.9
  9.9 214.4 %conditional.1 = (bf16[3584,3584]{1,0:T(8,128)(2,1)}, f32[3584]{0:T(1024)S(1)}, f32[3584]{0:T(1024)S(1)}) conditional(s32[]{:T(128)} %convert_element_type.50, (bf16[3584,3584]{1,0:T(8,128)(2,1)}, s32[2048]{0:T(1024)}, bf16[256,3584]{1,0:T(8,128)(2,1)}, bf16[512,3584]{1,0:T(8,128)(2,1)}) %tuple.19, (s32[]{:T(128)}, s32[1024]{0:T(1024)}, ...), branch_computations={%region_2.10_spmd, %region_10.15_spmd} | conditional | flops 53063917568 | bytes 343684800 | solution.py:383
  10.1 0.7 broadcast_compare_fusion.1
  10.9 1.5 convert_reduce_fusion
  12.3 0.6 select_reduce_fusion
  12.9 0.8 compare_convert_fusion.1.hot_a
  13.7 0.8 compare_convert_fusion.hot_b
  14.5 208.2 %branch_1_fun.1 = (bf16[3584,3584]{1,0:T(8,128)(2,1)}, f32[1,3584]{1,0:T(1,128)}, f32[1,3584]{1,0:T(1,128)}) custom-call(bf16[288,512]{1,0:T(8,128)(2,1)} %compare_convert_fusion.hot_b, bf16[288,256]{1,0:T(8,128)(2,1)} %compare_convert_fusion.1.hot_a, bf16[512,3584]{1,0:T(8,128)(2,1)} %get-tuple-element.40.store_b, ...), custom_call_target="tpu_custom_call" | custom-call | flops 26306674688 | bytes 51380224 | tf_op jit(solution)/shard_map/cond/branch_1_fun/pallas_call | solution.py:304
  222.7 0.8 reduce
  223.5 0.8 reduce.1
  224.3 0.0 copy-start.1
  224.3 0.0 copy-start.2
  224.3 20.8 %copy.20 = bf16[3584,3584]{1,0:T(8,128)(2,1)} copy(bf16[3584,3584]{1,0:T(8,128)(2,1)} %get-tuple-element.71) | data formatting | bytes 51380224
  245.1 0.0 copy-done.1
  245.1 0.0 copy-done.2
  (6 shorter events, 0.0 us)
Async XLA Ops:
  7.9 0.6 copy-start
  224.3 20.9 %copy-start.1 = (f32[3584]{0:T(1024)}, f32[3584]{0:T(1024)S(1)}, u32[]{:S(2)}) copy-start(f32[3584]{0:T(1024)S(1)} %get-tuple-element.72) | copy-start | bytes 43012
  224.3 20.8 %copy-start.2 = (f32[3584]{0:T(1024)}, f32[3584]{0:T(1024)S(1)}, u32[]{:S(2)}) copy-start(f32[3584]{0:T(1024)S(1)} %get-tuple-element.73) | copy-start | bytes 43012
